TPU v7x, 256 devices: a whole 4x4x8 slice. The times are simulated.
256 devices in a mesh: patch: 32 (over y, z_lo, x), head: 8 (over z_hi, core).
Axes of the slice: x: 4, y: 4, z: 8 (z_hi: 4, z_lo: 2; z = z_hi * 2 + z_lo), core: 2. Of those that a mesh axis runs over, the one named last changes fastest.
Arguments:
- fresh_qkv: bfloat16 [16384, 9216], P(('patch', 'head')), may hold values from -500 to 500
- stale_kv: bfloat16 [16384, 2, 3072], P('patch', None, 'head'), may hold values from -100 to 100
- qk_gain: float32 [2, 128], replicated, may hold values from 1 to 2
- patch_len: int32 [32], replicated, may hold values from 384 to 512, as said below
- gate_table: float32 [50, 3072], replicated, may hold values from 4 to 16
- timestep: int32 [1], replicated, may hold values from 0 to 49
Outputs:
- gated: bfloat16 [16384, 3072], P(('patch', 'head'))
Inputs may be any that keep to these rules, and one draw needn't show every extreme that they name: Positions of patch p at or past patch_len[p] are padding; some patch is full.
All inputs are finite; a program needn't handle non-finite values.
Results may differ from a plain program's by a relative error of at most 0.01.
Values may be sent and summed in bfloat16 or wider, within the bound.
A program may use at most 128 MiB of HBM per device.

v0:
```python
import math

import jax
import jax.numpy as jnp
from jax import lax
from jax.sharding import PartitionSpec as P

eps = 1e-06
neg_floor = -1e30


def normalize(values, gain):
    widened = values.astype(jnp.float32)
    inverse = lax.rsqrt(jnp.mean(widened * widened, axis=-1, keepdims=True) + eps)
    return (widened * inverse * gain).astype(jnp.bfloat16)


def update(softmax_state, queries, block_keys, block_values, key_live):
    running, denominator, numerator = softmax_state
    head_dim = queries.shape[-1]
    scores = jnp.einsum(
        "qhd,khd->qhk", queries, block_keys, preferred_element_type=jnp.float32
    ) * head_dim ** (-0.5)
    scores = jnp.where(key_live[None, None, :], scores, neg_floor)
    highest = jnp.maximum(running, jnp.max(scores, axis=-1))
    factor = jnp.exp(running - highest)
    weights = jnp.where(key_live[None, None, :], jnp.exp(scores - highest[..., None]), 0.0)
    denominator = denominator * factor + jnp.sum(weights, axis=-1)
    numerator = numerator * factor[..., None] + jnp.einsum(
        "qhk,khd->qhd",
        weights.astype(jnp.bfloat16),
        block_values,
        preferred_element_type=jnp.float32,
    )
    return (highest, denominator, numerator)


def sweep_keys(softmax_state, queries, all_keys, all_values, key_live):
    key_count = all_keys.shape[0]
    block_rows = math.gcd(key_count, 2048)
    if block_rows == key_count:
        return update(softmax_state, queries, all_keys, all_values, key_live)
    block_count = key_count // block_rows

    def one_block(carried, block_item):
        return (update(carried, queries, block_item[0], block_item[1], block_item[2]), None)

    blocked = (
        all_keys.reshape((block_count, block_rows) + all_keys.shape[1:]),
        all_values.reshape((block_count, block_rows) + all_values.shape[1:]),
        key_live.reshape(block_count, block_rows),
    )
    softmax_state, _ = lax.scan(one_block, softmax_state, blocked)
    return softmax_state


def local(fresh_qkv, stale_kv, qk_gain, patch_len, gate_table, timestep):
    groups = lax.axis_size("head")
    patch_count = lax.axis_size("patch")
    tok_dev = fresh_qkv.shape[0]
    head_dim = qk_gain.shape[1]
    group_width = stale_kv.shape[2]
    head_count = group_width // head_dim
    columns = fresh_qkv.reshape(tok_dev, 3, groups, group_width)
    regrouped = lax.all_to_all(columns, "head", split_axis=2, concat_axis=0, tiled=True)
    tok_patch = tok_dev * groups
    regrouped = regrouped.reshape(tok_patch, 3, head_count, head_dim)
    queries = normalize(regrouped[:, 0], qk_gain[0])
    fresh_keys = normalize(regrouped[:, 1], qk_gain[1])
    fresh_values = regrouped[:, 2]
    this_patch = lax.axis_index("patch")
    patch_ids = jnp.arange(patch_count, dtype=jnp.int32)
    own_length = jnp.sum(jnp.where(patch_ids == this_patch, patch_len, 0))
    fresh_live = jnp.arange(tok_patch, dtype=jnp.int32) < own_length
    blank_state = (
        jnp.full((tok_patch, head_count), neg_floor, jnp.float32),
        jnp.zeros((tok_patch, head_count), jnp.float32),
        jnp.zeros((tok_patch, head_count, head_dim), jnp.float32),
    )
    start_state = sweep_keys(blank_state, queries, fresh_keys, fresh_values, fresh_live)
    piece = lax.all_gather(stale_kv, "patch", axis=0, tiled=True)
    key_count = piece.shape[0]
    key_rows = jnp.arange(key_count, dtype=jnp.int32)
    source = key_rows // tok_patch
    position = key_rows % tok_patch
    key_limit = jnp.sum(
        jnp.where(source[:, None] == patch_ids[None, :], patch_len[None, :], 0), axis=1
    )
    key_live = (position < key_limit) & (source != this_patch)
    key_pair = piece.reshape(key_count, 2, head_count, head_dim)
    softmax_state = sweep_keys(start_state, queries, key_pair[:, 0], key_pair[:, 1], key_live)
    attended = (softmax_state[2] / softmax_state[1][..., None]).astype(jnp.bfloat16)
    attended = attended.reshape(tok_patch, 1, group_width)
    returned = lax.all_to_all(attended, "head", split_axis=0, concat_axis=1, tiled=True).reshape(
        tok_dev, groups * group_width
    )
    gate_row = lax.dynamic_slice_in_dim(gate_table, timestep[0], 1, 0)
    return (returned.astype(jnp.float32) * gate_row).astype(jnp.bfloat16)


def solution(mesh):
    return jax.shard_map(
        local,
        mesh=mesh,
        in_specs=(P(("patch", "head"), None), P("patch", None, "head"), P(), P(), P(), P()),
        out_specs=P(("patch", "head"), None),
        check_vma=False,
    )
```

profile of v0, /device:TPU:1, one launch (start us, length us, event | category | flops | bytes accessed | tf_op | source)
XLA Modules:
  0.0 498.2 jit_solution(9584098784748649941)
XLA Ops:
  6.5 3.2 copy.119
  9.7 0.0 all-gather.2.cloned.1.call-update
  9.7 0.0 copy-start.4
  9.8 0.0 copy-start.3
  9.8 0.2 copy.134
  10.0 1.3 copy.109
  11.3 10.0 %all-to-all-start = ((bf16[64,3,8,384]{3,0,1,2:T(8,128)(2,1)}), bf16[64,3,8,384]{3,0,1,2:T(8,128)(2,1)S(1)}, u32[]{:S(2)}, u32[]{:S(2)}) async-start(bf16[64,3,8,384]{3,0,1,2:T(8,128)(2,1)} %copy.109), calls=%async_computation | async-start | bytes 2359296 | tf_op jit(solution)/shard_map/all_to_all | solution.py:65
  21.3 0.5 select_reduce_fusion
  21.7 0.7 fusion.59
  22.4 0.6 iota_compare_fusion.1
  23.1 0.1 fusion.57
  23.2 38.6 %all-to-all-done = bf16[64,3,8,384]{3,0,1,2:T(8,128)(2,1)S(1)} async-done(((bf16[64,3,8,384]{3,0,1,2:T(8,128)(2,1)}), bf16[64,3,8,384]{3,0,1,2:T(8,128)(2,1)S(1)}, u32[]{:S(2)}, u32[]{:S(2)}) %all-to-all-start) | async-done | bytes 1179680 | tf_op jit(solution)/shard_map/all_to_all | solution.py:65
  61.8 1.2 copy.110
  63.0 3.3 reshape.82
  66.3 1.2 fusion.42
  67.5 0.1 add_rsqrt_fusion
  67.6 1.7 fusion.44
  69.3 0.1 copy.116
  69.3 0.0 slice-start
  69.3 0.6 bitcast_reduce_fusion.1
  70.0 0.9 fusion.31
  70.9 1.4 fusion.39
  72.3 0.3 copy.122
  72.5 243.6 %all-gather.2.cloned.1.call-done = bf16[16384,2,384]{0,2,1:T(8,128)(2,1)} async-done(((bf16[512,2,384]{0,2,1:T(8,128)(2,1)}), bf16[16384,2,384]{0,2,1:T(8,128)(2,1)}) %all-gather.2.cloned.1.call-update) | async-done | bytes 25165840 | tf_op jit(solution)/shard_map/all_gather | solution.py:81
  316.2 17.1 %fusion.64 = (bf16[16384,1,3,128]{0,3,2,1:T(8,128)(2,1)}, bf16[16384,1,3,128]{0,3,2,1:T(8,128)(2,1)}) fusion(bf16[16384,2,3,128]{0,3,2,1:T(8,128)(2,1)} %bitcast.124), kind=kLoop, calls=%fused_computation.91 | loop fusion | bytes 50331648 | tf_op jit(solution)/shard_map/slice | solution.py:91
  333.3 16.7 %copy.121 = bf16[16384,1,3,128]{3,0,2,1:T(8,128)(2,1)} copy(bf16[16384,1,3,128]{0,3,2,1:T(8,128)(2,1)} %get-tuple-element.136) | data formatting | bytes 25165824 | tf_op jit(solution)/shard_map/slice | solution.py:91
  350.0 16.5 %copy.120 = bf16[16384,1,3,128]{3,0,2,1:T(8,128)(2,1)} copy(bf16[16384,1,3,128]{0,3,2,1:T(8,128)(2,1)} %get-tuple-element.137) | data formatting | bytes 25165824 | tf_op jit(solution)/shard_map/slice | solution.py:91
  366.5 101.0 %while.14 = (s32[]{:T(128)}, f32[512,3]{0,1:T(4,128)S(1)}, f32[512,3]{0,1:T(4,128)S(1)}, f32[512,3,128]{0,2,1:T(8,128)S(1)}, pred[8,2048]{1,0:T(8,128)(4,1)S(1)}...) while((s32[]{:T(128)}, f32[512,3]{0,1:T(4,128)S(1)}, ...), condition=%wide.region_9.10_spmd, body=%wide.region_6.9_spmd.sunk | while | flops 1651903488 | bytes 42975344 | solution.py:53
  366.6 3.9 bitcast_reduce_fusion.3
  370.5 3.7 fusion.76
  374.2 4.9 fusion.77
  379.2 3.9 bitcast_reduce_fusion.3
  383.1 3.7 fusion.76
  386.8 4.9 fusion.77
  391.8 3.9 bitcast_reduce_fusion.3
  395.7 3.7 fusion.76
  399.5 4.9 fusion.77
  404.5 3.9 bitcast_reduce_fusion.3
  408.4 3.7 fusion.76
  412.1 4.9 fusion.77
  417.1 3.9 bitcast_reduce_fusion.3
  421.0 3.7 fusion.76
  424.7 4.9 fusion.77
  429.7 3.9 bitcast_reduce_fusion.3
  433.6 3.7 fusion.76
  437.4 4.9 fusion.77
  442.4 3.9 bitcast_reduce_fusion.3
  446.3 3.7 fusion.76
  450.0 4.9 fusion.77
  455.0 3.9 bitcast_reduce_fusion.3
  458.9 3.7 fusion.76
  462.6 4.9 fusion.77
  467.6 0.1 divide_convert_fusion
  467.7 0.5 broadcast.146
  468.2 0.9 reduce.2
  469.1 0.2 copy.145
  469.3 0.8 reshape.90
  470.2 6.9 %all-to-all-start.1 = ((bf16[8,2,12288]{2,1,0:T(2,128)(2,1)}), bf16[8,2,12288]{2,1,0:T(2,128)(2,1)S(1)}, u32[]{:S(2)}, u32[]{:S(2)}) async-start(bf16[8,2,12288]{2,1,0:T(2,128)(2,1)} %reshape.90), calls=%async_computation.1 | async-start | bytes 786432 | tf_op jit(solution)/shard_map/all_to_all | solution.py:94
  477.8 12.2 %all-to-all-done.1 = bf16[8,2,12288]{2,1,0:T(2,128)(2,1)S(1)} async-done(((bf16[8,2,12288]{2,1,0:T(2,128)(2,1)}), bf16[8,2,12288]{2,1,0:T(2,128)(2,1)S(1)}, u32[]{:S(2)}, u32[]{:S(2)}) %all-to-all-start.1) | async-done | bytes 393248 | tf_op jit(solution)/shard_map/all_to_all | solution.py:94
  490.0 0.4 reshape.91
  490.4 0.1 copy.127
  490.5 0.1 fusion.65
  490.5 0.1 copy.135
  490.6 0.8 multiply_convert_fusion
  (48 shorter events, 0.6 us)
Async XLA Ops:
  6.5 471.2 %copy-start = (f32[50,3072]{1,0:T(8,128)S(1)}, f32[50,3072]{1,0:T(8,128)}, u32[]{:S(2)}) copy-start(f32[50,3072]{1,0:T(8,128)} %param.12) | copy-start | bytes 1843204
  6.5 3.2 copy-start.2
  6.5 309.6 %all-gather.2.cloned.1.call-start = ((), (), s32[]{:S(2)}) async-start(), calls=%async_computation.2 | async-start | bytes 25952256 | tf_op jit(solution)/shard_map/all_gather | solution.py:81
  9.7 11.5 %copy-start.4 = (s32[32]{0:T(128)S(1)}, s32[32]{0:T(128)}, u32[]{:S(2)}) copy-start(s32[32]{0:T(128)} %param.11) | copy-start | bytes 388
  9.8 13.3 %copy-start.3 = (f32[2,128]{1,0:T(2,128)S(1)}, f32[2,128]{1,0:T(2,128)}, u32[]{:S(2)}) copy-start(f32[2,128]{1,0:T(2,128)} %param.10) | copy-start | bytes 3076
  11.3 50.5 %all-to-all-start = ((bf16[64,3,8,384]{3,0,1,2:T(8,128)(2,1)}), bf16[64,3,8,384]{3,0,1,2:T(8,128)(2,1)S(1)}, u32[]{:S(2)}, u32[]{:S(2)}) async-start(bf16[64,3,8,384]{3,0,1,2:T(8,128)(2,1)} %copy.109), calls=%async_computation | async-start | bytes 2359296 | tf_op jit(solution)/shard_map/all_to_all | solution.py:65
  66.3 2.9 copy-start.1
  69.3 1.6 slice-start
  470.2 19.8 %all-to-all-start.1 = ((bf16[8,2,12288]{2,1,0:T(2,128)(2,1)}), bf16[8,2,12288]{2,1,0:T(2,128)(2,1)S(1)}, u32[]{:S(2)}, u32[]{:S(2)}) async-start(bf16[8,2,12288]{2,1,0:T(2,128)(2,1)} %reshape.90), calls=%async_computation.1 | async-start | bytes 786432 | tf_op jit(solution)/shard_map/all_to_all | solution.py:94
Sparse Core Ops, SparseCore 0:
  9.9 306.2 all-gather.1
where the time goes:
time: 500 us; the launch traced here: 498 us
  waiting for transfers between devices  294 us (59%)
  matrix products  72.5 us (14%)
  local copies, waits for them, and re-layouts  62.4 us (12%)
  other arithmetic  37.3 us (7%)
  starting transfers between devices  16.9 us (3%)
  between operations  14.3 us (3%)
    all_gather x1, waiting for transfers between devices, local(): piece = lax.all_gather(stale_kv, 'patch', axis=0, tiled=True)  244 us
    dot_general x9, matrix products, update(): jnp.einsum('qhk,khd->qhd', weights.astype(jnp.bfloat16), block_values, pr...  40.8 us
    all_to_all x1, waiting for transfers between devices, local(): lax.all_to_all(columns, 'head', split_axis=2, concat_axis=0, tiled=True)  38.6 us
    slice x2, local copies, waits for them, and re-layouts, local(): key_pair[:, 1]  33.8 us
    dot_general x9, matrix products, update(): jnp.einsum('qhd,khd->qhk', queries, block_keys, preferred_element_type=jn...  31.7 us
    reduce_sum x9, other arithmetic, update(): denominator = denominator * factor + jnp.sum(weights, axis=-1)  30.4 us
    slice x1, local copies, waits for them, and re-layouts, local(): key_pair[:, 0]  16.5 us
    all_to_all x1, waiting for transfers between devices, local(): lax.all_to_all(attended, 'head', split_axis=0, concat_axis=1, tiled=True)  12.2 us
  transfers between devices with their start and end apart: 3, of which 3 were waited for; matrix products, arithmetic and copies ran while one was open for 3% of the time, Pallas kernels for 0%

commit v1 on v0

v1 whole, which is shorter than its diff:
```python
import functools
import math

import jax
import jax.numpy as jnp
from jax import lax
from jax.experimental import pallas as pl
from jax.experimental.pallas import tpu as pltpu
from jax.sharding import PartitionSpec as P

F32 = jnp.float32
BF16 = jnp.bfloat16
MESH = pl.DeviceIdType.MESH
EPS = 1e-06
DEAD = -1e30
HD = 128
TOK = 512
ROWS = 64
GROUPS = 8
NH = 3
WIDTH = 3072
SLOTS = 8
QS = 4
MSG = TOK + 32
TQ = 256
LIVE = 384
SCALE = math.log2(math.e) / math.sqrt(HD)
NT = (((1,), (1,)), ((), ()))


def kernel(
    fresh, stale, gain, lens, gate, out,
    qsend, ksend, qbuf, kbuf, vbuf, osend, orecv, att, ret, bias,
    s0, s1, p0, p1, m0, m1, otile, ltile,
    qa_s, qa_r, fa_s, fa_r, z_s, z_r, w_s, w_r, f_s, f_r, qg_s, qg_r, og_s, og_r, oa_s, oa_r, loc,
):
    patch = lax.axis_index("patch")
    g = lax.axis_index("head")
    core = lax.rem(g, 2)
    y, zl, x = patch // 8, lax.rem(patch // 4, 2), lax.rem(patch, 4)
    a = x + core * (y - x)
    b = y + core * (x - y)

    def place(a_, zl_, b_):
        return a_ * (1 + 7 * core) + b_ * (8 - 7 * core) + zl_ * 4

    def along_a(d):
        return (place(lax.rem(a + d, 4), zl, b), g)

    def along_b(d):
        return (place(a, zl, lax.rem(b + d, 4)), g)

    def group(d):
        return lax.rem(g + d, GROUPS)

    other_zl = (place(a, 1 - zl, b), g)

    lane = lax.broadcasted_iota(jnp.int32, (1, HD), 1) + LIVE
    for slot in range(SLOTS + 1):
        d, dz = (0, 0) if slot == SLOTS else (slot % 4, slot // 4)
        source = place(lax.rem(a + 4 - d, 4), lax.rem(zl + dz, 2), b)
        bias[slot : slot + 1, :] = jnp.where(lane < lens[source], 0.0, DEAD)

    def fill(i, _):
        rows = pl.ds(pl.multiple_of(i * TOK, TOK), TOK)
        for h in range(NH):
            vbuf[h, rows, HD:] = jnp.ones((TOK, HD), BF16)
        return 0

    lax.fori_loop(0, SLOTS + 1, fill, 0)

    barrier = pltpu.get_barrier_semaphore()
    peers = [(patch, group(d)) for d in range(1, GROUPS)]
    peers += [along_a(d) for d in range(1, 4)] + [along_b(d) for d in range(1, 4)] + [other_zl]
    for peer in peers:
        pl.semaphore_signal(barrier, inc=1, device_id=peer, device_id_type=MESH)
    pl.semaphore_wait(barrier, len(peers))

    def remote(src, dst, ss, rs, dev):
        return pltpu.make_async_remote_copy(
            src_ref=src, dst_ref=dst, send_sem=ss, recv_sem=rs, device_id=dev, device_id_type=MESH
        )

    def slot_rows(slot):
        return pl.ds(slot * TOK, TOK)

    def kv_slot(t, h, slot):
        return kbuf.at[h, slot_rows(slot)] if t == 0 else vbuf.at[h, slot_rows(slot), pl.ds(0, HD)]

    def zl_copy(t, h):
        return remote(stale.at[h, t], kv_slot(t, h, 4), z_s.at[h, t], z_r.at[h, t], other_zl)

    def own_copy(t, h, d):
        return remote(stale.at[h, t], kv_slot(t, h, d), w_s.at[h, t, d], w_r.at[h, t, d], along_a(d))

    def forward_copy(t, h, d):
        return remote(
            kv_slot(t, h, 4), kv_slot(t, h, 4 + d), f_s.at[h, t, d], f_r.at[h, t, d], along_a(d)
        )

    def columns(base, gg, h):
        return pl.ds(pl.multiple_of(base + (gg * NH + h) * HD, HD), HD)

    def token_rows(gg):
        return pl.ds(pl.multiple_of(gg * ROWS, ROWS), ROWS)

    def q_copy(h, d, src_g=None):
        to = group(d)
        return remote(
            qsend.at[:, columns(0, to, h)],
            qbuf.at[h, 0, token_rows(g if src_g is None else src_g)],
            qa_s.at[h, d], qa_r.at[h, d], (patch, to),
        )

    def fresh_copy(t, h, d, src_g=None):
        to = group(d)
        rows = token_rows(g if src_g is None else src_g)
        if t == 0:
            return remote(
                ksend.at[:, columns(0, to, h)], kbuf.at[h, rows],
                fa_s.at[h, t, d], fa_r.at[h, t, d], (patch, to),
            )
        return remote(
            fresh.at[:, columns(2 * WIDTH, to, h)], vbuf.at[h, rows, pl.ds(0, HD)],
            fa_s.at[h, t, d], fa_r.at[h, t, d], (patch, to),
        )

    def query_copy(h, d):
        return remote(qbuf.at[h, 0], qbuf.at[h, d], qg_s.at[h, d], qg_r.at[h, d], along_b(d))

    def partial_copy(h, d):
        return remote(
            osend.at[h, d - 1], orecv.at[h, d - 1], og_s.at[h, d], og_r.at[h, d], along_b(4 - d)
        )

    def out_copy(h, d, src_g=None):
        to = group(d)
        return remote(
            att.at[h, token_rows(to)],
            ret.at[:, columns(0, g if src_g is None else src_g, h)],
            oa_s.at[h, d], oa_r.at[h, d], (patch, to),
        )

    def arrived(copy_of, *args):
        d = args[-1]
        copy_of(*args, src_g=lax.rem(g + GROUPS - d, GROUPS)).wait_recv()

    def own_local(t, h):
        return pltpu.make_async_copy(stale.at[h, t], kv_slot(t, h, SLOTS), loc.at[h, t])

    def start_stale(h):
        for t in range(2):
            zl_copy(t, h).start()
        for d in (1, 3, 2):
            for t in range(2):
                own_copy(t, h, d).start()

    def start_forward(h):
        for t in range(2):
            zl_copy(t, h).wait_recv()
        for d in (1, 3, 2):
            for t in range(2):
                forward_copy(t, h, d).start()

    start_stale(0)

    def norm(base, which, dst):
        def one(i, _):
            cols = pl.ds(pl.multiple_of(base + i * HD, HD), HD)
            wide = fresh[:, cols].astype(F32)
            inverse = lax.rsqrt(jnp.mean(wide * wide, axis=-1, keepdims=True) + EPS)
            scaled = wide * inverse * gain[which : which + 1, :]
            dst[:, pl.ds(pl.multiple_of(i * HD, HD), HD)] = scaled.astype(BF16)
            return 0

        lax.fori_loop(0, GROUPS * NH, one, 0)

    norm(0, 0, qsend)
    for h in range(NH):
        for d in range(1, GROUPS):
            q_copy(h, d).start()
        qbuf[h, 0, token_rows(g), :] = qsend[:, columns(0, g, h)]
    start_stale(1)
    norm(WIDTH, 1, ksend)
    for h in range(NH):
        kbuf[h, token_rows(g), :] = ksend[:, columns(0, g, h)]
        vbuf[h, token_rows(g), 0:HD] = fresh[:, columns(2 * WIDTH, g, h)]
        for t in range(2):
            own_local(t, h).start()

    def start_queries(h):
        for d in range(1, GROUPS):
            arrived(q_copy, h, d)
        for d in range(1, 4):
            query_copy(h, d).start()

    start_queries(0)
    start_forward(0)
    start_stale(2)
    for h in range(1, NH):
        start_queries(h)
    for h in range(NH):
        for t in range(2):
            for d in range(1, GROUPS):
                fresh_copy(t, h, d).start()
    for h in range(NH):
        for t in range(2):
            own_local(t, h).wait()

    def await_keys(h):
        for t in range(2):
            for d in range(1, 4):
                own_copy(t, h, d).wait_recv()
                forward_copy(t, h, d).wait_recv()

    def await_fresh(h):
        for t in range(2):
            for d in range(1, GROUPS):
                arrived(fresh_copy, t, h, d)

    n_far = NH * (QS - 1)
    n_units = NH * QS

    def unit(u):
        own = u >= n_far
        h = jnp.where(own, u - n_far, u // (QS - 1))
        j = jnp.where(own, 0, lax.rem(u, QS - 1) + 1)
        return h, j, jnp.where(own, 0, 1)

    def score(h, j, first, r, s_ref, m_ref):
        q = qbuf[h, j, r : r + TQ, :]
        top = None
        for s in range(SLOTS):
            rows = pl.ds(pl.multiple_of((first + s) * TOK, TOK), TOK)
            sc = lax.dot_general(q, kbuf[h, rows, :], NT, preferred_element_type=F32)
            parts = [sc[:, i * HD : (i + 1) * HD] for i in range(TOK // HD)]
            parts[-1] = parts[-1] + bias[pl.ds(first + s, 1), :]
            for i, part in enumerate(parts):
                s_ref[:, s * TOK + i * HD : s * TOK + (i + 1) * HD] = part
                top = part if top is None else jnp.maximum(top, part)
        m_ref[...] = jnp.broadcast_to(jnp.max(top, axis=1, keepdims=True) * SCALE, (TQ, HD))

    def weigh(h, first, r, s_ref, m_ref, p_ref):
        high = m_ref[...]
        for i in range(SLOTS * TOK // HD):
            cols = slice(i * HD, (i + 1) * HD)
            p_ref[:, cols] = jnp.exp2(s_ref[:, cols] * SCALE - high).astype(BF16)
        rows = pl.ds(pl.multiple_of(first * TOK, TOK), SLOTS * TOK)
        both = jnp.dot(p_ref[...], vbuf[h, rows, :], preferred_element_type=F32)
        total = both[:, HD:]
        otile[r : r + TQ, :] = both[:, :HD] / total
        ltile[r : r + TQ, :] = high + jnp.log2(total)

    diagonal = lax.broadcasted_iota(jnp.int32, (HD, HD), 0) == lax.broadcasted_iota(
        jnp.int32, (HD, HD), 1
    )

    def send_partial(h, j):
        osend[h, j - 1, 0:TOK, :] = otile[...].astype(BF16)
        logs = jnp.concatenate(
            [
                jnp.sum(jnp.where(diagonal, ltile[i * HD : (i + 1) * HD, :], 0.0), axis=0, keepdims=True)
                for i in range(TOK // HD)
            ]
            + [jnp.zeros((4, HD), F32)],
            axis=0,
        )
        high = logs.astype(BF16).astype(F32)
        middle = (logs - high).astype(BF16).astype(F32)
        low = logs - high - middle
        packed = jnp.concatenate([high, middle, low, jnp.zeros((8, HD), F32)], axis=0)
        osend[h, j - 1, TOK:MSG, :] = packed.astype(BF16)
        partial_copy(h, j).start()

    def merge(h):
        logs = []
        for d in range(1, QS):
            partial_copy(h, d).wait_recv()
            packed = orecv[h, d - 1, TOK:MSG, :].astype(F32)
            logs.append(packed[0:8] + packed[8:16] + packed[16:24])
        for i in range(TOK // HD):
            rows = slice(i * HD, (i + 1) * HD)
            spread = [ltile[rows, :]] + [
                jnp.transpose(jnp.broadcast_to(log[i : i + 1, :], (HD, HD))) for log in logs
            ]
            top = functools.reduce(jnp.maximum, spread)
            shares = [jnp.exp2(one - top) for one in spread]
            total = functools.reduce(jnp.add, shares)
            mixed = shares[0] * otile[rows, :]
            for d in range(1, QS):
                mixed = mixed + shares[d] * orecv[h, d - 1, rows, :].astype(F32)
            att[h, rows, :] = (mixed / total).astype(BF16)
        for d in range(1, GROUPS):
            out_copy(h, d).start()
        ret[:, columns(0, g, h)] = att[h, token_rows(g), :]

    await_keys(0)
    query_copy(0, 1).wait_recv()
    score(0, 1, 1, 0, s0, m0)

    def step(u, _):
        h, j, first = unit(u)
        later = jnp.minimum(u + 1, n_units - 1)
        h2, j2, first2 = unit(later)

        @pl.when(u == 0)
        def _():
            start_forward(1)

        @pl.when(u == 2)
        def _():
            start_forward(2)

        score(h, j, first, TQ, s1, m1)
        weigh(h, first, 0, s0, m0, p0)

        @pl.when(u + 1 < n_far)
        def _():
            query_copy(h2, j2).wait_recv()

        @pl.when((u + 1 < n_far) & (j2 == 1))
        def _():
            await_keys(h2)

        @pl.when((u + 1 >= n_far) & (u + 1 < n_units))
        def _():
            await_fresh(h2)

        score(h2, j2, first2, 0, s0, m0)
        weigh(h, first, TQ, s1, m1, p1)

        @pl.when(u < n_far)
        def _():
            send_partial(h, j)

        @pl.when(u >= n_far)
        def _():
            merge(h)

        return 0

    lax.fori_loop(0, n_units, step, 0)

    for h in range(NH):
        for d in range(1, GROUPS):
            arrived(out_copy, h, d)
    out[...] = (ret[...].astype(F32) * gate[...]).astype(BF16)

    for h in range(NH):
        for d in range(1, GROUPS):
            q_copy(h, d).wait_send()
            out_copy(h, d).wait_send()
            for t in range(2):
                fresh_copy(t, h, d).wait_send()
        for t in range(2):
            zl_copy(t, h).wait_send()
            for d in range(1, 4):
                own_copy(t, h, d).wait_send()
                forward_copy(t, h, d).wait_send()
        for d in range(1, 4):
            query_copy(h, d).wait_send()
            partial_copy(h, d).wait_send()


def local(fresh_qkv, stale_kv, qk_gain, patch_len, gate_table, timestep):
    stale = stale_kv.reshape(TOK, 2, NH, HD).transpose(2, 1, 0, 3)
    gate = lax.dynamic_slice_in_dim(gate_table, timestep[0], 1, 0)
    dma = pltpu.SemaphoreType.DMA
    vmem = pl.BlockSpec(memory_space=pltpu.VMEM)
    keys = (SLOTS + 1) * TOK
    return pl.pallas_call(
        kernel,
        out_shape=jax.ShapeDtypeStruct((ROWS, WIDTH), BF16),
        in_specs=[vmem, vmem, vmem, pl.BlockSpec(memory_space=pltpu.SMEM), vmem],
        out_specs=vmem,
        scratch_shapes=[
            pltpu.VMEM((ROWS, WIDTH), BF16),
            pltpu.VMEM((ROWS, WIDTH), BF16),
            pltpu.VMEM((NH, QS, TOK, HD), BF16),
            pltpu.VMEM((NH, keys, HD), BF16),
            pltpu.VMEM((NH, keys, 2 * HD), BF16),
            pltpu.VMEM((NH, QS - 1, MSG, HD), BF16),
            pltpu.VMEM((NH, QS - 1, MSG, HD), BF16),
            pltpu.VMEM((NH, TOK, HD), BF16),
            pltpu.VMEM((ROWS, WIDTH), BF16),
            pltpu.VMEM((16, HD), F32),
            pltpu.VMEM((TQ, SLOTS * TOK), F32),
            pltpu.VMEM((TQ, SLOTS * TOK), F32),
            pltpu.VMEM((TQ, SLOTS * TOK), BF16),
            pltpu.VMEM((TQ, SLOTS * TOK), BF16),
            pltpu.VMEM((TQ, HD), F32),
            pltpu.VMEM((TQ, HD), F32),
            pltpu.VMEM((TOK, HD), F32),
            pltpu.VMEM((TOK, HD), F32),
            dma((NH, GROUPS)), dma((NH, GROUPS)),
            dma((NH, 2, GROUPS)), dma((NH, 2, GROUPS)),
            dma((NH, 2)), dma((NH, 2)),
            dma((NH, 2, 4)), dma((NH, 2, 4)),
            dma((NH, 2, 4)), dma((NH, 2, 4)),
            dma((NH, 4)), dma((NH, 4)),
            dma((NH, 4)), dma((NH, 4)),
            dma((NH, GROUPS)), dma((NH, GROUPS)),
            dma((NH, 2)),
        ],
        compiler_params=pltpu.CompilerParams(
            collective_id=0, has_side_effects=True, vmem_limit_bytes=56 << 20
        ),
    )(fresh_qkv, stale, qk_gain, patch_len, gate)


def solution(mesh):
    return jax.shard_map(
        local,
        mesh=mesh,
        in_specs=(P(("patch", "head"), None), P("patch", None, "head"), P(), P(), P(), P()),
        out_specs=P(("patch", "head"), None),
        check_vma=False,
    )
```

time: 500 us -> 101 us (0.20)
  waiting for transfers between devices: 294 us -> 0 us
  Pallas kernels: 0 us -> 94.2 us
  matrix products: 72.5 us -> 0 us
  local copies, waits for them, and re-layouts: 62.4 us -> 5.86 us
  other arithmetic: 37.3 us -> 0 us
  starting transfers between devices: 16.9 us -> 0 us
  between operations: 14.3 us -> 0.68 us
    all_gather x1 -> x0, waiting for transfers between devices: 244 us -> none  [local(): piece = lax.all_gather(stale_kv, 'patch', axis=0, tiled=True)]
    pallas_call x0 -> x1, Pallas kernels: none -> 94.2 us  [local(): pl.pallas_call(kernel, out_shape=jax.ShapeDtypeStruct((ROWS, WIDTH), BF16...]
    dot_general x18 -> x0, matrix products: 72.5 us -> none  [the longest x9 40.8 us: update(): jnp.einsum('qhk,khd->qhd', weights.astype(jnp.bfloat16), block_values, pr...]
    all_to_all x2 -> x0, waiting for transfers between devices: 50.8 us -> none  [the longest x1 38.6 us: local(): lax.all_to_all(columns, 'head', split_axis=2, concat_axis=0, tiled=True)]
    slice x5 -> x0, local copies, waits for them, and re-layouts: 50.4 us -> none  [the longest x2 33.8 us: local(): key_pair[:, 1]]
    reduce_sum x12 -> x0, other arithmetic: 32.7 us -> none  [the longest x9 30.4 us: update(): denominator = denominator * factor + jnp.sum(weights, axis=-1)]
    all_to_all x2 -> x0, starting transfers between devices: 16.9 us -> none  [the longest x1 9.97 us: local(): lax.all_to_all(columns, 'head', split_axis=2, concat_axis=0, tiled=True)]
  transfers between devices with their start and end apart: 3 -> 0, of which waited for: 3 -> 0; matrix products, arithmetic and copies ran while one was open for 3% -> 0% of each run, Pallas kernels for 0% -> 0%
where the time goes in v1:
time: 101 us
  Pallas kernels  94.2 us (93%)
  local copies, waits for them, and re-layouts  5.86 us (6%)
    pallas_call x1, Pallas kernels, local(): pl.pallas_call(kernel, out_shape=jax.ShapeDtypeStruct((ROWS, WIDTH), BF16...  94.2 us
    unnamed x4, local copies, waits for them, and re-layouts  4.09 us

profile of v1, /device:TPU:1, one launch (start us, length us, event | category | flops | bytes accessed | tf_op | source)
XLA Modules:
  0.0 100.7 jit_solution(7167847819030074281)
XLA Ops:
  0.0 0.0 copy-start
  0.0 2.3 %copy.7 = bf16[512,2,384]{0,2,1:T(8,128)(2,1)S(1)} copy(bf16[512,2,384]{2,1,0:T(2,128)(2,1)} %param.7) | data formatting | bytes 1572864 | tf_op args[1]
  2.3 1.2 %copy.8 = bf16[512,2,3,128]{3,0,1,2:T(8,128)(2,1)} copy(bf16[512,2,3,128]{0,3,2,1:T(8,128)(2,1)S(1)} %bitcast.6) | data formatting | bytes 1572864 | tf_op jit(solution)/shard_map/reshape | solution.py:366
  4.1 0.0 copy-done
  4.2 0.6 constant_dynamic-slice_fusion.gate
  4.8 94.2 %shard_map.64 = bf16[64,3072]{1,0:T(8,128)(2,1)} custom-call(bf16[64,9216]{1,0:T(8,128)(2,1)} %fresh.1, bf16[3,2,512,128]{3,2,1,0:T(8,128)(2,1)} %bitcast.7, f32[2,128]{1,0:T(2,128)} %gain.1, s32[32]{0:T(128)} %lens.1, f32[1,3072]{1,0:T(1,128)} %constant_dynamic-slice_fusion.gate), custom_call_target="tpu_custom_call" | custom-call | tf_op jit(solution)/shard_map/pallas_call | solution.py:371
  98.9 1.8 %copy.11 = bf16[64,3072]{1,0:T(8,128)(2,1)} copy(bf16[64,3072]{1,0:T(8,128)(2,1)} %shard_map.64) | data formatting | bytes 786432
Async XLA Ops:
  0.0 4.1 %copy-start = (f32[50,3072]{1,0:T(8,128)S(1)}, f32[50,3072]{1,0:T(8,128)}, u32[]{:S(2)}) copy-start(f32[50,3072]{1,0:T(8,128)} %param.10) | copy-start | bytes 1843204

commit v2 on v1

v2 whole, which is shorter than its diff:
```python
import functools
import math

import jax
import jax.numpy as jnp
from jax import lax
from jax.experimental import pallas as pl
from jax.experimental.pallas import tpu as pltpu
from jax.sharding import PartitionSpec as P

F32 = jnp.float32
BF16 = jnp.bfloat16
MESH = pl.DeviceIdType.MESH
EPS = 1e-06
DEAD = -1e30
HD = 128
TOK = 512
ROWS = 64
GROUPS = 8
NH = 3
WIDTH = 3072
SLOTS = 9
QS = 4
MSG = TOK + 32
CHUNK = 4
OWN = 4
FAR = 5
LIVE = 384
SCALE = math.log2(math.e) / math.sqrt(HD)
NT = (((1,), (1,)), ((), ()))


def kernel(
    fresh, stale, gain, lens, out,
    qsend, ksend, qbuf, kbuf, vbuf, osend, orecv, att, ret, bias,
    s0, s1, p0, p1, m0, m1, otile, ltile, ohalf, lhalf,
    qa_s, qa_r, fa_s, fa_r, z_s, z_r, w_s, w_r, f_s, f_r, qg_s, qg_r, og_s, og_r, oa_s, oa_r,
):
    patch = lax.axis_index("patch")
    g = lax.axis_index("head")
    core = lax.rem(g, 2)
    y, zl, x = patch // 8, lax.rem(patch // 4, 2), lax.rem(patch, 4)
    a = x + core * (y - x)
    b = y + core * (x - y)

    def place(a_, zl_, b_):
        return a_ * (1 + 7 * core) + b_ * (8 - 7 * core) + zl_ * 4

    def along_a(d):
        return (place(lax.rem(a + d, 4), zl, b), g)

    def along_b(d):
        return (place(a, zl, lax.rem(b + d, 4)), g)

    def group(d):
        return lax.rem(g + d, GROUPS)

    other_zl = (place(a, 1 - zl, b), g)

    barrier = pltpu.get_barrier_semaphore()
    peers = [(patch, group(d)) for d in range(1, GROUPS)]
    peers += [along_a(d) for d in range(1, 4)] + [along_b(d) for d in range(1, 4)] + [other_zl]
    for peer in peers:
        pl.semaphore_signal(barrier, inc=1, device_id=peer, device_id_type=MESH)

    def slot_rows(slot):
        return pl.ds(slot * TOK, TOK)

    def split(h):
        cols = slice(h * HD, (h + 1) * HD)
        kbuf[h, slot_rows(OWN), :] = stale[:, 0, cols]
        vbuf[h, slot_rows(OWN), 0:HD] = stale[:, 1, cols]

    def norm(base, which, dst):
        def one(i, _):
            cols = pl.ds(pl.multiple_of(base + i * HD, HD), HD)
            wide = fresh[:, cols].astype(F32)
            inverse = lax.rsqrt(jnp.mean(wide * wide, axis=-1, keepdims=True) + EPS)
            scaled = wide * inverse * gain[which : which + 1, :]
            dst[:, pl.ds(pl.multiple_of(i * HD, HD), HD)] = scaled.astype(BF16)
            return 0

        lax.fori_loop(0, GROUPS * NH, one, 0)

    split(0)
    norm(0, 0, qsend)
    lane = lax.broadcasted_iota(jnp.int32, (1, HD), 1) + LIVE
    for slot in range(SLOTS):
        d, dz = (slot % OWN, 0) if slot < FAR else (slot - FAR, 1)
        source = place(lax.rem(a + 4 - d, 4), lax.rem(zl + dz, 2), b)
        bias[slot : slot + 1, :] = jnp.where(lane < lens[source], 0.0, DEAD)

    def fill(i, _):
        rows = pl.ds(pl.multiple_of(i * TOK, TOK), TOK)
        for h in range(NH):
            vbuf[h, rows, HD:] = jnp.ones((TOK, HD), BF16)
        return 0

    lax.fori_loop(0, SLOTS, fill, 0)
    pl.semaphore_wait(barrier, len(peers))

    def remote(src, dst, ss, rs, dev):
        return pltpu.make_async_remote_copy(
            src_ref=src, dst_ref=dst, send_sem=ss, recv_sem=rs, device_id=dev, device_id_type=MESH
        )

    def kv_slot(t, h, slot):
        return kbuf.at[h, slot_rows(slot)] if t == 0 else vbuf.at[h, slot_rows(slot), pl.ds(0, HD)]

    def zl_copy(t, h):
        return remote(kv_slot(t, h, OWN), kv_slot(t, h, FAR), z_s, z_r.at[h, t], other_zl)

    def side_copy(t, h, d, far):
        ss, rs = (f_s, f_r) if far else (w_s, w_r)
        src, dst = (FAR, FAR + d) if far else (OWN, d)
        return remote(kv_slot(t, h, src), kv_slot(t, h, dst), ss, rs.at[h, t, d], along_a(d))

    def relay_copy(t, h):
        d = (1, 3)[t]
        return remote(kv_slot(t, h, d), kv_slot(t, h, 2), w_s, w_r.at[h, t, 2], along_a(d))

    def columns(base, gg, h):
        return pl.ds(pl.multiple_of(base + (gg * NH + h) * HD, HD), HD)

    def token_rows(gg):
        return pl.ds(pl.multiple_of(gg * ROWS, ROWS), ROWS)

    def q_copy(h, d):
        to = group(d)
        return remote(
            qsend.at[:, columns(0, to, h)], qbuf.at[h, 0, token_rows(g)], qa_s, qa_r.at[h], (patch, to)
        )

    def fresh_copy(t, h, d):
        to = group(d)
        rows = token_rows(g)
        if t == 0:
            src, dst = ksend.at[:, columns(0, to, h)], kbuf.at[h, rows]
        else:
            src, dst = fresh.at[:, columns(2 * WIDTH, to, h)], vbuf.at[h, rows, pl.ds(0, HD)]
        return remote(src, dst, fa_s.at[t], fa_r.at[h, t], (patch, to))

    def query_copy(h, d):
        return remote(qbuf.at[h, 0], qbuf.at[h, d], qg_s, qg_r.at[h, d], along_b(d))

    def partial_copy(h, d):
        return remote(osend.at[h, d - 1], orecv.at[h, d - 1], og_s, og_r.at[h, d], along_b(4 - d))

    def out_copy(h, d):
        to = group(d)
        return remote(
            att.at[h, token_rows(to)], ret.at[:, columns(0, g, h)], oa_s, oa_r.at[h], (patch, to)
        )

    def wait_all(ref, sem):
        pltpu.make_async_copy(ref, ref, sem).wait()

    others = (GROUPS - 1) * ROWS

    def start_zl(h):
        for t in range(2):
            zl_copy(t, h).start()

    def start_side(h, far):
        for t in range(2):
            for d in (1, 3, 2) if far else (1, 3):
                side_copy(t, h, d, far).start()

    def start_relay(h):
        side_copy(0, h, 1, 0).wait_recv()
        relay_copy(0, h).start()
        side_copy(1, h, 3, 0).wait_recv()
        relay_copy(1, h).start()

    def start_forward(h):
        for t in range(2):
            zl_copy(t, h).wait_recv()
        start_side(h, 1)

    def start_q(h):
        for d in range(1, GROUPS):
            q_copy(h, d).start()

    def start_queries(h):
        wait_all(qbuf.at[h, 0, pl.ds(0, others)], qa_r.at[h])
        for d in (1, 3, 2):
            query_copy(h, d).start()

    def start_fresh(h):
        for t in range(2):
            for d in range(1, GROUPS):
                fresh_copy(t, h, d).start()

    for h in range(NH):
        start_q(h)
        if h < 2:
            start_side(h, 0)
        if h == 0:
            split(1)
            split(2)
    for h in range(NH):
        start_zl(h)
    norm(WIDTH, 1, ksend)
    for h in range(NH):
        start_fresh(h)
    for h in range(NH):
        qbuf[h, 0, token_rows(g), :] = qsend[:, columns(0, g, h)]
        kbuf[h, token_rows(g), :] = ksend[:, columns(0, g, h)]
        vbuf[h, token_rows(g), 0:HD] = fresh[:, columns(2 * WIDTH, g, h)]
    start_relay(0)
    start_queries(0)
    start_side(2, 0)
    start_relay(1)

    events = {
        0: [(start_queries, 1)],
        1: [(start_relay, 2)],
        2: [(start_queries, 2)],
        3: [(start_forward, 0)],
        6: [(start_forward, 1)],
        9: [(start_forward, 2)],
    }

    def await_keys(h, far):
        side_copy(0, h, 3, far).wait_recv()
        side_copy(1, h, 1, far).wait_recv()
        if far:
            side_copy(0, h, 1, far).wait_recv()
            side_copy(1, h, 3, far).wait_recv()
        for t in range(2):
            side_copy(t, h, 2, far).wait_recv()

    def await_fresh(h):
        wait_all(kbuf.at[h, pl.ds(0, others)], fa_r.at[h, 0])
        wait_all(vbuf.at[h, pl.ds(0, others), pl.ds(0, HD)], fa_r.at[h, 1])

    n_half = NH * (QS - 1)
    n_own = 2 * n_half
    n_steps = 2 * NH * QS

    def unit(t):
        own = t >= n_own
        far = jnp.where(own, lax.rem(t - n_own, 2), t // n_half)
        r = lax.rem(t, n_half)
        h = jnp.where(own, (t - n_own) // 2, r // (QS - 1))
        j = jnp.where(own, 0, lax.rem(r, QS - 1) + 1)
        first = jnp.where(far == 1, FAR, jnp.where(own, 0, 1))
        return h, j, first, far

    def score(h, j, first, s_ref, m_ref):
        q = qbuf[h, j]
        top = None
        for s in range(CHUNK):
            rows = pl.ds(pl.multiple_of((first + s) * TOK, TOK), TOK)
            sc = lax.dot_general(q, kbuf[h, rows, :], NT, preferred_element_type=F32)
            parts = [sc[:, i * HD : (i + 1) * HD] for i in range(TOK // HD)]
            parts[-1] = parts[-1] + bias[pl.ds(first + s, 1), :]
            for i, part in enumerate(parts):
                s_ref[:, s * TOK + i * HD : s * TOK + (i + 1) * HD] = part
                top = part if top is None else jnp.maximum(top, part)
        m_ref[...] = jnp.broadcast_to(jnp.max(top, axis=1, keepdims=True) * SCALE, (TOK, HD))

    def weigh(h, first, s_ref, m_ref, p_ref):
        high = m_ref[...]
        for i in range(CHUNK * TOK // HD):
            cols = slice(i * HD, (i + 1) * HD)
            p_ref[:, cols] = jnp.exp2(s_ref[:, cols] * SCALE - high).astype(BF16)
        rows = pl.ds(pl.multiple_of(first * TOK, TOK), CHUNK * TOK)
        both = jnp.dot(p_ref[...], vbuf[h, rows, :], preferred_element_type=F32)
        total = both[:, HD:]
        otile[...] = both[:, :HD] / total
        ltile[...] = high + jnp.log2(total)

    def join(h, j):
        near, here = lhalf[h, j], ltile[...]
        top = jnp.maximum(near, here)
        w_near, w_here = jnp.exp2(near - top), jnp.exp2(here - top)
        total = w_near + w_here
        otile[...] = (w_near * ohalf[h, j] + w_here * otile[...]) / total
        ltile[...] = top + jnp.log2(total)

    diagonal = lax.broadcasted_iota(jnp.int32, (HD, HD), 0) == lax.broadcasted_iota(
        jnp.int32, (HD, HD), 1
    )

    def send_partial(h, j):
        osend[h, j - 1, 0:TOK, :] = otile[...].astype(BF16)
        logs = jnp.concatenate(
            [
                jnp.sum(jnp.where(diagonal, ltile[i * HD : (i + 1) * HD, :], 0.0), axis=0, keepdims=True)
                for i in range(TOK // HD)
            ]
            + [jnp.zeros((4, HD), F32)],
            axis=0,
        )
        high = logs.astype(BF16).astype(F32)
        middle = (logs - high).astype(BF16).astype(F32)
        low = logs - high - middle
        packed = jnp.concatenate([high, middle, low, jnp.zeros((8, HD), F32)], axis=0)
        osend[h, j - 1, TOK:MSG, :] = packed.astype(BF16)
        partial_copy(h, j).start()

    def merge(h):
        logs = []
        for d in range(1, QS):
            partial_copy(h, d).wait_recv()
            packed = orecv[h, d - 1, TOK:MSG, :].astype(F32)
            logs.append(packed[0:8] + packed[8:16] + packed[16:24])
        for i in range(TOK // HD):
            rows = slice(i * HD, (i + 1) * HD)
            spread = [ltile[rows, :]] + [
                jnp.transpose(jnp.broadcast_to(log[i : i + 1, :], (HD, HD))) for log in logs
            ]
            top = functools.reduce(jnp.maximum, spread)
            shares = [jnp.exp2(one - top) for one in spread]
            total = functools.reduce(jnp.add, shares)
            mixed = shares[0] * otile[rows, :]
            for d in range(1, QS):
                mixed = mixed + shares[d] * orecv[h, d - 1, rows, :].astype(F32)
            att[h, rows, :] = (mixed / total).astype(BF16)
        for d in range(1, GROUPS):
            out_copy(h, d).start()
        ret[:, columns(0, g, h)] = att[h, token_rows(g), :]

    def await_inputs(t, h, j, far):
        @pl.when((t < n_half) & (j == 1))
        def _():
            await_keys(h, 0)

        @pl.when(t < n_half)
        def _():
            query_copy(h, j).wait_recv()

        @pl.when((t >= n_half) & (t < n_own) & (j == 1))
        def _():
            await_keys(h, 1)

        @pl.when((t >= n_own) & (far == 0))
        def _():
            await_fresh(h)

    def finish(h, j, far):
        @pl.when(far == 0)
        def _():
            ohalf[h, j] = otile[...]
            lhalf[h, j] = ltile[...]

        @pl.when((far == 1) & (j > 0))
        def _():
            join(h, j)
            send_partial(h, j)

        @pl.when((far == 1) & (j == 0))
        def _():
            join(h, j)
            merge(h)

    await_keys(0, 0)
    query_copy(0, 1).wait_recv()
    score(0, 1, 1, s0, m0)

    def pair(u, _):
        for half, (s_in, m_in, p, s_out, m_out) in enumerate(((s0, m0, p0, s1, m1), (s1, m1, p1, s0, m0))):
            t = 2 * u + half
            for when, calls in events.items():
                if when % 2 == half:

                    @pl.when(u == when // 2)
                    def _(calls=calls):
                        for call, *args in calls:
                            call(*args)

            h, j, first, far = unit(t)
            later = t + 1
            if half == 1:
                later = jnp.minimum(later, n_steps - 1)
            h2, j2, first2, far2 = unit(later)
            if half == 1:

                @pl.when(t + 1 < n_steps)
                def _():
                    await_inputs(later, h2, j2, far2)

            else:
                await_inputs(later, h2, j2, far2)
            score(h2, j2, first2, s_out, m_out)
            weigh(h, first, s_in, m_in, p)
            finish(h, j, far)
        return 0

    lax.fori_loop(0, n_steps // 2, pair, 0)

    for h in range(NH):
        wait_all(att.at[h, pl.ds(0, others)], oa_r.at[h])
    out[...] = ret[...]

    wait_all(kbuf.at[0, pl.ds(0, NH * others)], qa_s)
    for t in range(2):
        wait_all(kbuf.at[0, pl.ds(0, NH * others)], fa_s.at[t])
    wait_all(kbuf.at[0, pl.ds(0, NH * others)], oa_s)
    wait_all(kbuf.at[0, pl.ds(0, NH * 2 * TOK)], z_s)
    wait_all(kbuf.at[pl.ds(0, 2)], w_s)
    wait_all(kbuf.at[pl.ds(0, 2)], f_s)
    wait_all(kbuf.at[0], qg_s)
    wait_all(orecv, og_s)


def local(fresh_qkv, stale_kv, qk_gain, patch_len, gate_table, timestep):
    dma = pltpu.SemaphoreType.DMA
    vmem = pl.BlockSpec(memory_space=pltpu.VMEM)
    keys = SLOTS * TOK
    returned = pl.pallas_call(
        kernel,
        out_shape=jax.ShapeDtypeStruct((ROWS, WIDTH), BF16),
        in_specs=[vmem, vmem, vmem, pl.BlockSpec(memory_space=pltpu.SMEM)],
        out_specs=vmem,
        scratch_shapes=[
            pltpu.VMEM((ROWS, WIDTH), BF16),
            pltpu.VMEM((ROWS, WIDTH), BF16),
            pltpu.VMEM((NH, QS, TOK, HD), BF16),
            pltpu.VMEM((NH, keys, HD), BF16),
            pltpu.VMEM((NH, keys, 2 * HD), BF16),
            pltpu.VMEM((NH, QS - 1, MSG, HD), BF16),
            pltpu.VMEM((NH, QS - 1, MSG, HD), BF16),
            pltpu.VMEM((NH, TOK, HD), BF16),
            pltpu.VMEM((ROWS, WIDTH), BF16),
            pltpu.VMEM((16, HD), F32),
            pltpu.VMEM((TOK, CHUNK * TOK), F32),
            pltpu.VMEM((TOK, CHUNK * TOK), F32),
            pltpu.VMEM((TOK, CHUNK * TOK), BF16),
            pltpu.VMEM((TOK, CHUNK * TOK), BF16),
            pltpu.VMEM((TOK, HD), F32),
            pltpu.VMEM((TOK, HD), F32),
            pltpu.VMEM((TOK, HD), F32),
            pltpu.VMEM((TOK, HD), F32),
            pltpu.VMEM((NH, QS, TOK, HD), F32),
            pltpu.VMEM((NH, QS, TOK, HD), F32),
            dma, dma((NH,)),
            dma((2,)), dma((NH, 2)),
            dma, dma((NH, 2)),
            dma, dma((NH, 2, 4)),
            dma, dma((NH, 2, 4)),
            dma, dma((NH, 4)),
            dma, dma((NH, 4)),
            dma, dma((NH,)),
        ],
        compiler_params=pltpu.CompilerParams(
            collective_id=0, has_side_effects=True, vmem_limit_bytes=56 << 20
        ),
    )(fresh_qkv, stale_kv, qk_gain, patch_len)
    gate_row = lax.dynamic_slice_in_dim(gate_table, timestep[0], 1, 0)
    return (returned.astype(F32) * gate_row).astype(BF16)


def solution(mesh):
    return jax.shard_map(
        local,
        mesh=mesh,
        in_specs=(P(("patch", "head"), None), P("patch", None, "head"), P(), P(), P(), P()),
        out_specs=P(("patch", "head"), None),
        check_vma=False,
    )
```

time: 101 us -> 90.3 us (0.89)
  Pallas kernels: 94.2 us -> 87.1 us
  local copies, waits for them, and re-layouts: 5.86 us -> 0.4 us
  other arithmetic: 0 us -> 1.81 us
    pallas_call x1, Pallas kernels: 94.2 us -> 87.1 us  [local(): pl.pallas_call(kernel, out_shape=jax.ShapeDtypeStruct((ROWS, WIDTH), BF16...]
    unnamed x4 -> x2, local copies, waits for them, and re-layouts: 4.09 us -> 0.39 us
    convert_element_type x0 -> x1, other arithmetic: none -> 1.81 us  [local(): return (returned.astype(F32) * gate_row).astype(BF16)]
    reshape x1 -> x0, local copies, waits for them, and re-layouts: 1.16 us -> none  [local(): stale = stale_kv.reshape(TOK, 2, NH, HD).transpose(2, 1, 0, 3)]
where the time goes in v2:
time: 90.3 us; the launch traced here: 90.1 us
  Pallas kernels  87.1 us (96%)
  other arithmetic  1.81 us (2%)
    pallas_call x1, Pallas kernels, local(): pl.pallas_call(kernel, out_shape=jax.ShapeDtypeStruct((ROWS, WIDTH), BF16...  87.1 us
    convert_element_type x1, other arithmetic, local(): return (returned.astype(F32) * gate_row).astype(BF16)  1.81 us

profile of v2, /device:TPU:1, one launch (start us, length us, event | category | flops | bytes accessed | tf_op | source)
XLA Modules:
  0.0 90.1 jit_solution(14960525164471853643)
XLA Ops:
  0.0 0.0 copy-start
  0.7 0.4 copy-done
  1.1 87.1 %shard_map.64 = bf16[64,3072]{1,0:T(8,128)(2,1)} custom-call(bf16[64,9216]{1,0:T(8,128)(2,1)} %fresh.1, bf16[512,2,384]{2,1,0:T(2,128)(2,1)} %stale.1, f32[2,128]{1,0:T(2,128)} %gain.1, s32[32]{0:T(128)} %lens.1), custom_call_target="tpu_custom_call" | custom-call | tf_op jit(solution)/shard_map/pallas_call | solution.py:412
  88.3 1.8 %multiply_convert_fusion = bf16[64,3072]{1,0:T(8,128)(2,1)} fusion(bf16[64,3072]{1,0:T(8,128)(2,1)} %shard_map.64, f32[3072]{0:T(1024)S(1)} %bitcast.5), kind=kLoop, calls=%fused_computation | loop fusion | flops 589824 | bytes 798720 | tf_op jit(solution)/shard_map/convert_element_type | solution.py:452
  (1 shorter events, 0.0 us)
Async XLA Ops:
  0.0 1.1 %copy-start = (f32[50,3072]{1,0:T(8,128)S(1)}, f32[50,3072]{1,0:T(8,128)}, u32[]{:S(2)}) copy-start(f32[50,3072]{1,0:T(8,128)} %param.10) | copy-start | bytes 1843204

commit v3 on v2

--- a/solution.py
+++ b/solution.py
@@ -33,7 +33,7 @@
 def kernel(
     fresh, stale, gain, lens, out,
     qsend, ksend, qbuf, kbuf, vbuf, osend, orecv, att, ret, bias,
-    s0, s1, p0, p1, m0, m1, otile, ltile, ohalf, lhalf,
+    s0, s1, p0, p1, m0, m1, otile, ltile, ohalf, lhalf, kstage, vstage,
     qa_s, qa_r, fa_s, fa_r, z_s, z_r, w_s, w_r, f_s, f_r, qg_s, qg_r, og_s, og_r, oa_s, oa_r,
 ):
     patch = lax.axis_index("patch")
@@ -131,14 +131,11 @@
             qsend.at[:, columns(0, to, h)], qbuf.at[h, 0, token_rows(g)], qa_s, qa_r.at[h], (patch, to)
         )
 
-    def fresh_copy(t, h, d):
+    def fresh_copy(t, d):
         to = group(d)
-        rows = token_rows(g)
-        if t == 0:
-            src, dst = ksend.at[:, columns(0, to, h)], kbuf.at[h, rows]
-        else:
-            src, dst = fresh.at[:, columns(2 * WIDTH, to, h)], vbuf.at[h, rows, pl.ds(0, HD)]
-        return remote(src, dst, fa_s.at[t], fa_r.at[h, t], (patch, to))
+        base, src, dst = ((0, ksend, kstage), (2 * WIDTH, fresh, vstage))[t]
+        cols = pl.ds(pl.multiple_of(base + to * (NH * HD), HD), NH * HD)
+        return remote(src.at[:, cols], dst.at[token_rows(g)], fa_s.at[t], fa_r.at[t], (patch, to))
 
     def query_copy(h, d):
         return remote(qbuf.at[h, 0], qbuf.at[h, d], qg_s, qg_r.at[h, d], along_b(d))
@@ -186,30 +183,32 @@
         for d in (1, 3, 2):
             query_copy(h, d).start()
 
-    def start_fresh(h):
+    def start_fresh():
         for t in range(2):
             for d in range(1, GROUPS):
-                fresh_copy(t, h, d).start()
-
-    for h in range(NH):
-        start_q(h)
-        if h < 2:
-            start_side(h, 0)
-        if h == 0:
-            split(1)
-            split(2)
+                fresh_copy(t, d).start()
+
+    start_q(0)
+    start_side(0, 0)
+    start_q(1)
+    qbuf[0, 0, token_rows(g), :] = qsend[:, columns(0, g, 0)]
+    split(1)
+    start_side(1, 0)
+    split(2)
+    start_q(2)
+    start_relay(0)
+    start_queries(0)
     for h in range(NH):
         start_zl(h)
+    start_side(2, 0)
     norm(WIDTH, 1, ksend)
+    start_fresh()
     for h in range(NH):
-        start_fresh(h)
-    for h in range(NH):
-        qbuf[h, 0, token_rows(g), :] = qsend[:, columns(0, g, h)]
-        kbuf[h, token_rows(g), :] = ksend[:, columns(0, g, h)]
-        vbuf[h, token_rows(g), 0:HD] = fresh[:, columns(2 * WIDTH, g, h)]
-    start_relay(0)
-    start_queries(0)
-    start_side(2, 0)
+        if h > 0:
+            qbuf[h, 0, token_rows(g), :] = qsend[:, columns(0, g, h)]
+        cols = columns(0, g, h)
+        kstage[token_rows(g), h * HD : (h + 1) * HD] = ksend[:, cols]
+        vstage[token_rows(g), h * HD : (h + 1) * HD] = fresh[:, columns(2 * WIDTH, g, h)]
     start_relay(1)
 
     events = {
@@ -230,9 +229,13 @@
         for t in range(2):
             side_copy(t, h, 2, far).wait_recv()
 
-    def await_fresh(h):
-        wait_all(kbuf.at[h, pl.ds(0, others)], fa_r.at[h, 0])
-        wait_all(vbuf.at[h, pl.ds(0, others), pl.ds(0, HD)], fa_r.at[h, 1])
+    def await_fresh():
+        wait_all(kstage.at[pl.ds(0, others)], fa_r.at[0])
+        wait_all(vstage.at[pl.ds(0, others)], fa_r.at[1])
+        for h in range(NH):
+            cols = slice(h * HD, (h + 1) * HD)
+            kbuf[h, 0:TOK, :] = kstage[:, cols]
+            vbuf[h, 0:TOK, 0:HD] = vstage[:, cols]
 
     n_half = NH * (QS - 1)
     n_own = 2 * n_half
@@ -335,9 +338,9 @@
         def _():
             await_keys(h, 1)
 
-        @pl.when((t >= n_own) & (far == 0))
-        def _():
-            await_fresh(h)
+        @pl.when(t == n_own)
+        def _():
+            await_fresh()
 
     def finish(h, j, far):
         @pl.when(far == 0)
@@ -396,7 +399,7 @@
 
     wait_all(kbuf.at[0, pl.ds(0, NH * others)], qa_s)
     for t in range(2):
-        wait_all(kbuf.at[0, pl.ds(0, NH * others)], fa_s.at[t])
+        wait_all(kstage.at[pl.ds(0, others)], fa_s.at[t])
     wait_all(kbuf.at[0, pl.ds(0, NH * others)], oa_s)
     wait_all(kbuf.at[0, pl.ds(0, NH * 2 * TOK)], z_s)
     wait_all(kbuf.at[pl.ds(0, 2)], w_s)
@@ -435,8 +438,10 @@
             pltpu.VMEM((TOK, HD), F32),
             pltpu.VMEM((NH, QS, TOK, HD), F32),
             pltpu.VMEM((NH, QS, TOK, HD), F32),
+            pltpu.VMEM((TOK, NH * HD), BF16),
+            pltpu.VMEM((TOK, NH * HD), BF16),
             dma, dma((NH,)),
-            dma((2,)), dma((NH, 2)),
+            dma((2,)), dma((2,)),
             dma, dma((NH, 2)),
             dma, dma((NH, 2, 4)),
             dma, dma((NH, 2, 4)),

time: 90.3 us -> 86.3 us (0.956)
  the two profiles are of different devices: /device:TPU:1 before, /device:TPU:27 now
where the time goes in v3:
time: 86.3 us; the launch traced here: 86.1 us
  Pallas kernels  83.2 us (96%)
  other arithmetic  1.81 us (2%)
    pallas_call x1, Pallas kernels, local(): pl.pallas_call(kernel, out_shape=jax.ShapeDtypeStruct((ROWS, WIDTH), BF16...  83.2 us
    convert_element_type x1, other arithmetic, local(): return (returned.astype(F32) * gate_row).astype(BF16)  1.81 us

profile of v3, /device:TPU:27, one launch (start us, length us, event | category | flops | bytes accessed | tf_op | source)
XLA Modules:
  0.0 86.1 jit_solution(12668510184704199691)
XLA Ops:
  0.0 0.0 copy-start
  0.7 0.4 copy-done
  1.1 83.2 %shard_map.64 = bf16[64,3072]{1,0:T(8,128)(2,1)} custom-call(bf16[64,9216]{1,0:T(8,128)(2,1)} %fresh.1, bf16[512,2,384]{2,1,0:T(2,128)(2,1)} %stale.1, f32[2,128]{1,0:T(2,128)} %gain.1, s32[32]{0:T(128)} %lens.1), custom_call_target="tpu_custom_call" | custom-call | tf_op jit(solution)/shard_map/pallas_call | solution.py:415
  84.3 1.8 %multiply_convert_fusion = bf16[64,3072]{1,0:T(8,128)(2,1)} fusion(bf16[64,3072]{1,0:T(8,128)(2,1)} %shard_map.64, f32[3072]{0:T(1024)S(1)} %bitcast.5), kind=kLoop, calls=%fused_computation | loop fusion | flops 589824 | bytes 798720 | tf_op jit(solution)/shard_map/convert_element_type | solution.py:457
  (1 shorter events, 0.0 us)
Async XLA Ops:
  0.0 1.1 %copy-start = (f32[50,3072]{1,0:T(8,128)S(1)}, f32[50,3072]{1,0:T(8,128)}, u32[]{:S(2)}) copy-start(f32[50,3072]{1,0:T(8,128)} %param.10) | copy-start | bytes 1843204

commit v4 on v3

--- a/solution.py
+++ b/solution.py
@@ -213,9 +213,8 @@
 
     events = {
         0: [(start_queries, 1)],
-        1: [(start_relay, 2)],
         2: [(start_queries, 2)],
-        3: [(start_forward, 0)],
+        3: [(start_relay, 2), (start_forward, 0)],
         6: [(start_forward, 1)],
         9: [(start_forward, 2)],
     }

time: 86.3 us -> 86.1 us (level)
  the two profiles are of different devices: /device:TPU:27 before, /device:TPU:1 now
where the time goes in v4:
time: 86.1 us; the launch traced here: 85.2 us
  Pallas kernels  82.3 us (96%)
  other arithmetic  1.81 us (2%)
    pallas_call x1, Pallas kernels, local(): pl.pallas_call(kernel, out_shape=jax.ShapeDtypeStruct((ROWS, WIDTH), BF16...  82.3 us
    convert_element_type x1, other arithmetic, local(): return (returned.astype(F32) * gate_row).astype(BF16)  1.81 us

profile of v4, /device:TPU:1, one launch (start us, length us, event | category | flops | bytes accessed | tf_op | source)
XLA Modules:
  0.0 85.2 jit_solution(2248116131251476767)
XLA Ops:
  0.0 0.0 copy-start
  0.7 0.4 copy-done
  1.1 82.3 %shard_map.64 = bf16[64,3072]{1,0:T(8,128)(2,1)} custom-call(bf16[64,9216]{1,0:T(8,128)(2,1)} %fresh.1, bf16[512,2,384]{2,1,0:T(2,128)(2,1)} %stale.1, f32[2,128]{1,0:T(2,128)} %gain.1, s32[32]{0:T(128)} %lens.1), custom_call_target="tpu_custom_call" | custom-call | tf_op jit(solution)/shard_map/pallas_call | solution.py:414
  83.4 1.8 %multiply_convert_fusion = bf16[64,3072]{1,0:T(8,128)(2,1)} fusion(bf16[64,3072]{1,0:T(8,128)(2,1)} %shard_map.64, f32[3072]{0:T(1024)S(1)} %bitcast.5), kind=kLoop, calls=%fused_computation | loop fusion | flops 589824 | bytes 798720 | tf_op jit(solution)/shard_map/convert_element_type | solution.py:456
  (1 shorter events, 0.0 us)
Async XLA Ops:
  0.0 1.1 %copy-start = (f32[50,3072]{1,0:T(8,128)S(1)}, f32[50,3072]{1,0:T(8,128)}, u32[]{:S(2)}) copy-start(f32[50,3072]{1,0:T(8,128)} %param.10) | copy-start | bytes 1843204
